TPU v7x, 128 devices: a whole 4x4x4 slice. The times are simulated.
128 devices in a mesh: dp: 16 (over z_hi, x, core), tensor: 8 (over z_lo, y).
Axes of the slice: x: 4, y: 4, z: 4 (z_hi: 2, z_lo: 2; z = z_hi * 2 + z_lo), core: 2. Of those that a mesh axis runs over, the one named last changes fastest.
Arguments:
- query: bfloat16 [16384, 8192], P('dp', 'tensor'), may hold values from -17 to 17
- key_resp: bfloat16 [16384, 1024], P('dp', 'tensor'), may hold values from -4 to 4
- value_resp: bfloat16 [16384, 1024], P('dp', 'tensor'), may hold values from -4 to 4
- d_hidden: bfloat16 [16384, 5120], P('dp', 'tensor'), may hold values from -6 to 6
- w_out: bfloat16 [8192, 5120], P('tensor'), may hold values from -0.0625 to 0.0625
- prompt_key: bfloat16 [8192, 1024], P('dp', 'tensor'), may hold values from -4 to 4
- prompt_value: bfloat16 [8192, 1024], P('dp', 'tensor'), may hold values from -4 to 4
- response_group: int32 [64], P('dp'), may hold values from 0 to 15, as said below
- response_length: int32 [64], P('dp'), may hold values from 32 to 256, as said below
- prompt_owner: int32 [16], replicated, may hold values from 0 to 15, each once
Outputs:
- d_query: bfloat16 [16384, 8192], P('dp', 'tensor')
- d_key_resp: bfloat16 [16384, 1024], P('dp', 'tensor')
- d_value_resp: bfloat16 [16384, 1024], P('dp', 'tensor')
- d_prompt_key: bfloat16 [8192, 1024], P('dp', 'tensor')
- d_prompt_value: bfloat16 [8192, 1024], P('dp', 'tensor')
Inputs may be any that keep to these rules, and one draw needn't show every extreme that they name: `response_group`: each group number is named by exactly 4 responses. `response_length`: the real tokens of each response; the later of its 256 slots are padding.
All inputs are finite; a program needn't handle non-finite values.
Results may differ from a plain program's by a relative error of at most 0.0067.
Values may be sent and summed in bfloat16 or wider, within the bound.
A program may use at most 192 MiB of HBM per device.

v0:
```python
import functools

import jax
import jax.numpy as jnp
from jax import lax
from jax.experimental import pallas as pl
from jax.experimental.pallas import tpu as pltpu
from jax.sharding import PartitionSpec as P

HEADS_DEV = 8
HD = 128
PROMPT = 512
LEN = 256
KEYS = PROMPT + LEN
RESP = 4
N_DP = 16
SHARD = 640
PIECE = PROMPT // N_DP
EXTRA = 16
HPI = 4
HALVES = HEADS_DEV // HPI
WIDE = HPI * LEN
SCALE = HD ** (-0.5)
SCALE_LOG2E = SCALE * 1.4426950408889634
f32, bf16 = jnp.float32, jnp.bfloat16
NT = (((1,), (1,)), ((), ()))
NN = (((1,), (0,)), ((), ()))

CUT_LO, CUT_P, CUT_HI = 80, 176, 192


def dotf(a, b, dims=NN):
    return lax.dot_general(a, b, dims, preferred_element_type=f32)


def kernel(
    group_ref, length_ref, owner_ref, q_in, k_in, v_in, h_in, w_in, pk_in, pv_in,
    dq_out, dk_out, dv_out, dpk_out, dpv_out,
    dh, w, q, g, dq, ko, vo, dko, dvo, tab, ka, va, kt, gacc, pb, prb, dsb, dka, dva, ctr, rbk, rbv, fin, frec, idx_v, idx_s,
    lsem, osem, d_send, d_recv, p_send, p_recv, a_send, a_recv, f_send, f_recv,
):
    dp = lax.axis_index("dp")
    ten = lax.axis_index("tensor")
    y, zl = lax.rem(ten, 4), ten // 4
    core, x, zh = lax.rem(dp, 2), lax.rem(dp // 2, 4), dp // 8

    def at_t(z_, y_):
        return z_ * 4 + lax.rem(y_ + 4, 4)

    def at_d(zh_, x_, c_):
        return zh_ * 8 + lax.rem(x_ + 4, 4) * 2 + c_

    t_plus, t_minus, t_z = at_t(zl, y + 1), at_t(zl, y - 1), at_t(1 - zl, y)
    d_plus, d_minus = at_d(zh, x + 1, core), at_d(zh, x - 1, core)
    d_zh, d_core = at_d(1 - zh, x, core), at_d(zh, x, 1 - core)
    place, place_zh = zh * 4 + x, (1 - zh) * 4 + x

    def cols(t_):
        return pl.ds(pl.multiple_of(t_ * SHARD, 128), SHARD)

    mine = [
        pltpu.make_async_copy(h_in, dh.at[:, cols(ten)], lsem.at[0]),
        pltpu.make_async_copy(pk_in, tab.at[0, place, core, 0:PROMPT], lsem.at[1]),
        pltpu.make_async_copy(pv_in, tab.at[1, place, core, 0:PROMPT], lsem.at[2]),
        pltpu.make_async_copy(q_in, q, lsem.at[3]),
        pltpu.make_async_copy(k_in, ko, lsem.at[4]),
        pltpu.make_async_copy(v_in, vo, lsem.at[5]),
        pltpu.make_async_copy(w_in, w, lsem.at[6]),
    ]
    for one in mine:
        one.start()

    slots = [owner_ref[group_ref[j]] for j in range(RESP)]
    row = lax.broadcasted_iota(jnp.int32, (EXTRA, HD), 0)
    filled = jnp.full((EXTRA, HD), -100, jnp.int32)
    for j in range(RESP):
        filled = jnp.where(row == j, slots[j], filled)
    for i in range(2):
        tab[i, place, core, PROMPT:] = filled.astype(f32).astype(bf16)

    barrier = pltpu.get_barrier_semaphore()
    for t_ in (t_plus, t_minus, t_z):
        pl.semaphore_signal(barrier, inc=1, device_id={"tensor": t_}, device_id_type=pl.DeviceIdType.MESH)
    for d_ in (d_plus, d_minus, d_zh, d_core):
        pl.semaphore_signal(barrier, inc=1, device_id={"dp": d_}, device_id_type=pl.DeviceIdType.MESH)
    for one in mine[:3]:
        one.wait()
    pl.semaphore_wait(barrier, 7)

    def send(src, dst, ss, rs, axis, target):
        pltpu.make_async_remote_copy(
            src_ref=src, dst_ref=dst, send_sem=ss, recv_sem=rs, device_id={axis: target},
            device_id_type=pl.DeviceIdType.MESH,
        ).start()

    def landed(ref, sem):
        pltpu.make_async_copy(ref, ref, sem).wait()

    def far(z_, y_):
        return at_t(z_, y_)

    nz = 1 - zl
    messages = [
        (ten, far(zl, y - 1), 0, LEN, t_plus),
        (ten, far(zl, y + 1), 0, LEN, t_minus),
        (ten, t_z, 0, LEN, t_z),
        (t_z, far(nz, y - 1), 0, CUT_P, t_plus),
        (t_z, far(nz, y + 1), 0, CUT_P, t_minus),
        (t_minus, far(zl, y + 2), CUT_LO, CUT_HI, t_plus),
        (t_plus, far(zl, y + 2), 0, CUT_LO, t_minus),
        (t_plus, far(zl, y + 2), CUT_HI, LEN, t_minus),
        (t_minus, far(nz, y - 1), CUT_P, LEN, t_z),
        (t_plus, far(nz, y + 1), CUT_P, LEN, t_z),
        (far(nz, y - 1), far(nz, y + 2), CUT_LO, CUT_P, t_plus),
        (far(nz, y + 1), far(nz, y + 2), 0, CUT_LO, t_minus),
        (far(zl, y + 2), far(nz, y + 2), CUT_P, CUT_HI, t_z),
        (far(zl, y + 2), far(nz, y + 2), CUT_HI, LEN, t_z),
    ]
    steps = ((0, 3), (3, 10), (10, 14))

    def part(c, shard, lo, hi):
        return dh.at[pl.ds(pl.multiple_of(c * LEN + lo, 16), hi - lo), cols(shard)]

    def h_send(c, step):
        for m in range(*steps[step]):
            source, _, lo, hi, target = messages[m]
            block = part(c, source, lo, hi)
            send(block, block, d_send.at[c, m], d_recv.at[c, m], "tensor", target)

    def h_wait(c, step):
        for m in range(*steps[step]):
            _, got, lo, hi, _ = messages[m]
            landed(part(c, got, lo, hi), d_recv.at[c, m])

    def h_done(c):
        for m in range(len(messages)):
            source, _, lo, hi, _ = messages[m]
            landed(part(c, source, lo, hi), d_send.at[c, m])

    def pair(p_, c_):
        return tab.at[:, p_, c_]

    def spot(zh_, x_):
        return zh_ * 4 + lax.rem(x_ + 4, 4)

    nh = 1 - zh

    def line(zh_, c_):
        return tab.at[:, pl.ds(zh_ * 4, 4), c_]

    prompts = [
        (pair(place, core), pair(place_zh, core), d_zh),
        (pair(place, core), pair(spot(zh, x - 1), core), d_plus),
        (pair(place, core), pair(spot(zh, x + 1), core), d_minus),
        (pair(place_zh, core), pair(spot(nh, x - 1), core), d_plus),
        (pair(place_zh, core), pair(spot(nh, x + 1), core), d_minus),
        (tab.at[0, spot(zh, x - 1), core], tab.at[0, spot(zh, x + 2), core], d_plus),
        (tab.at[1, spot(zh, x + 1), core], tab.at[1, spot(zh, x + 2), core], d_minus),
        (tab.at[0, spot(nh, x - 1), core], tab.at[0, spot(nh, x + 2), core], d_plus),
        (tab.at[1, spot(nh, x + 1), core], tab.at[1, spot(nh, x + 2), core], d_minus),
        (line(zh, core), line(zh, 1 - core), d_core),
        (line(nh, core), line(nh, 1 - core), d_core),
    ]

    def p_go(*which):
        for m in which:
            block, _, target = prompts[m]
            send(block, block, p_send.at[m], p_recv.at[m], "dp", target)

    def p_wait(*which):
        for m in which:
            landed(prompts[m][1], p_recv.at[m])

    def spread(block, landing, ss, rs):
        for k in range(1, N_DP):
            peer = lax.rem(dp + k, N_DP)
            send(block(peer), landing, ss, rs, "dp", peer)
        pltpu.make_async_copy(block(dp), landing, rs).start()

    p_go(0, 1, 2)
    h_send(0, 0)
    h_send(1, 0)
    p_wait(1, 2)
    p_go(5, 6)
    h_wait(0, 0)
    h_send(0, 1)
    p_wait(0)
    p_go(3, 4)

    h_wait(1, 0)
    h_send(2, 0)
    p_wait(3, 4)
    p_go(7, 8)
    p_wait(5, 6)
    p_go(9)
    h_wait(0, 1)
    h_send(0, 2)
    h_send(1, 1)
    p_wait(7, 8)
    p_go(10)
    for one in mine[3:]:
        one.wait()
    p_wait(9, 10)


    by_row = tab[0, :, :, PROMPT:].astype(f32)[:, :, 0:8].reshape(128, 128)
    by_lane = by_row.T
    i_row = lax.broadcasted_iota(jnp.int32, (128, 128), 0)
    i_lane = lax.broadcasted_iota(jnp.int32, (128, 128), 1)
    before = jnp.where((by_row == by_lane) & (i_row < i_lane), 1.0, 0.0)
    rank = jnp.sum(before, 0, keepdims=True)
    rank = jnp.broadcast_to(4.0 * by_lane[0:1] + rank, (64, 128))
    number = (lax.shift_right_logical(i_lane, 3) * RESP + (i_lane & 7)).astype(f32)
    hit = jnp.where(rank == i_row[:64].astype(f32), number[:64], 0.0)
    index = jnp.sum(hit, 1, keepdims=True)
    idx_v[...] = jnp.broadcast_to(index, (64, 128)).astype(jnp.int32)
    to_s = pltpu.make_async_copy(idx_v, idx_s, lsem.at[0])
    to_s.start()

    key_at = lax.broadcasted_iota(jnp.int32, (LEN, WIDE), 0)
    row_at = lax.rem(lax.broadcasted_iota(jnp.int32, (LEN, WIDE), 1), LEN)
    causal = key_at <= row_at
    t_at = lax.broadcasted_iota(jnp.int32, (HEADS_DEV * HD, LEN), 1)

    t_last = far(nz, y + 2)

    def gather_part(c):
        rows = pl.ds(pl.multiple_of(c * LEN, LEN), LEN)
        gacc[...] = jnp.zeros_like(gacc)

        @pl.loop(1, 8)
        def _(n):
            t_ = cols(lax.rem(t_last + n, 8))
            gacc[...] += dotf(w[:, t_], dh[rows, t_], NT)

    gather_part(0)

    def give(c, i):
        spread(lambda k: ctr.at[c, i, k], (rbk, rbv)[i].at[c, dp], a_send.at[c, i], a_recv.at[c, i])

    def add_up(i):
        for c in range(RESP):
            landed((rbk, rbv)[i].at[c], a_recv.at[c, i])

        @pl.loop(1, N_DP + 1)
        def _(n):
            s = lax.rem(dp + n, N_DP)
            total = jnp.zeros((PIECE, HD), f32)
            for k in range(RESP):
                r = idx_s[s * RESP + k, 0]
                total += (rbk, rbv)[i][r & (RESP - 1), lax.shift_right_logical(r, 2) & (N_DP - 1)].astype(f32)
            fin[i, s] = total.astype(bf16)
            landing = frec.at[i, pl.ds(dp * PIECE, PIECE)]

            @pl.when(n < N_DP)
            def _():
                send(fin.at[i, s], landing, f_send.at[i], f_recv.at[i], "dp", s)

            @pl.when(n == N_DP)
            def _():
                pltpu.make_async_copy(fin.at[i, s], landing, f_recv.at[i]).start()

    @pl.loop(0, RESP)
    def _(c):
        rows = pl.ds(pl.multiple_of(c * LEN, LEN), LEN)

        def heads(ref, h):
            return jnp.concatenate(
                [ref[rows, pl.ds(pl.multiple_of((h * HPI + i) * HD, HD), HD)] for i in range(HPI)], 0
            )

        length = length_ref[c]
        slot = owner_ref[group_ref[c]]
        spot_slot = lax.shift_right_logical(slot, 1) & 7
        ka[0:PROMPT] = tab[0, spot_slot, slot & 1, 0:PROMPT]
        va[0:PROMPT] = tab[1, spot_slot, slot & 1, 0:PROMPT]
        ka[PROMPT:KEYS] = ko[rows]
        va[PROMPT:KEYS] = vo[rows]
        kt[...] = ka[...].astype(f32).T.astype(bf16)
        dka[...] = jnp.zeros_like(dka)
        dva[...] = jnp.zeros_like(dva)

        @pl.loop(0, HALVES)
        def _(h):
            s = dotf(ka[...], heads(q, h), NT)
            so = jnp.where(causal, s[PROMPT:], -jnp.inf)
            sp = s[:PROMPT]
            m = jnp.maximum(jnp.max(sp, 0, keepdims=True), jnp.max(so, 0, keepdims=True))
            ep = jnp.exp2((sp - m) * SCALE_LOG2E)
            eo = jnp.exp2((so - m) * SCALE_LOG2E)
            inv = 1.0 / (jnp.sum(ep, 0, keepdims=True) + jnp.sum(eo, 0, keepdims=True))
            p = jnp.concatenate([ep * inv, eo * inv], 0)
            pb[h] = p
            prb[h] = p.astype(bf16)

        h_wait(c, 2)

        @pl.when(c <= 1)
        def _():
            h_wait(c + 2, 0)

        @pl.when(c == 0)
        def _():
            h_send(3, 0)

        grad = gacc[...] + dotf(w[:, cols(t_last)], dh[rows, cols(t_last)], NT)
        g[rows, :] = jnp.where(t_at < length, grad, 0.0).T.astype(bf16)

        @pl.loop(0, HALVES)
        def _(h):
            dva[...] += dotf(prb[h], heads(g, h))

        ctr[c, 1] = dva[0:PROMPT].astype(bf16).reshape(N_DP, PIECE, HD)
        give(c, 1)

        @pl.loop(0, HALVES)
        def _(h):
            d = dotf(va[...], heads(g, h), NT)
            delta = jnp.sum(prb[h].astype(f32) * d, 0, keepdims=True)
            ds = (pb[h] * (d - delta)).astype(bf16)
            dsb[h] = ds
            dka[...] += dotf(ds, heads(q, h))

        ctr[c, 0] = (dka[0:PROMPT] * SCALE).astype(bf16).reshape(N_DP, PIECE, HD)
        give(c, 0)

        @pl.when(c <= 2)
        def _():
            h_wait(c + 1, 1)
            h_send(c + 1, 2)

        @pl.when(c <= 1)
        def _():
            h_send(c + 2, 1)

        @pl.when(c <= 2)
        def _():
            gather_part(c + 1)

        @pl.when(c == RESP - 1)
        def _():
            to_s.wait()
            add_up(1)

        @pl.loop(0, HALVES)
        def _(h):
            dqt = dotf(kt[...], dsb[h]) * SCALE
            for i in range(HPI):
                head = pl.ds(pl.multiple_of((h * HPI + i) * HD, HD), HD)
                dq[rows, head] = dqt[:, i * LEN : (i + 1) * LEN].T.astype(bf16)

        dko[rows] = (dka[PROMPT:KEYS] * SCALE).astype(bf16)
        dvo[rows] = dva[PROMPT:KEYS].astype(bf16)
        for n, (block, out) in enumerate(((dq, dq_out), (dko, dk_out), (dvo, dv_out))):
            pltpu.make_async_copy(block.at[rows], out.at[rows], osem.at[c, n]).start()

    add_up(0)
    for c in range(RESP):
        h_done(c)
        for i in range(2):
            landed(ctr.at[c, i, 0:15], a_send.at[c, i])
        done = pl.ds(c * LEN, LEN)
        for n, (block, out) in enumerate(((dq, dq_out), (dko, dk_out), (dvo, dv_out))):
            pltpu.make_async_copy(block.at[done], out.at[done], osem.at[c, n]).wait()
    for m, (block, _, _) in enumerate(prompts):
        landed(block, p_send.at[m])
    last = [
        pltpu.make_async_copy(frec.at[1], dpv_out, lsem.at[1]),
        pltpu.make_async_copy(frec.at[0], dpk_out, lsem.at[2]),
    ]
    for i in (1, 0):
        landed(frec.at[i], f_recv.at[i])
        last[1 - i].start()
    for i in (1, 0):
        landed(fin.at[i, 0:15], f_send.at[i])
        last[1 - i].wait()


def hand_over(*refs):
    n = (len(refs) - 2) // 3
    sources, targets, held, sem_in, sem_out = refs[:n], refs[n : 2 * n], refs[2 * n : 3 * n], refs[-2], refs[-1]
    parts = [(i, pl.ds(k * LEN, LEN)) for i in range(n) for k in range(sources[i].shape[0] // LEN if i == 0 else 1)]
    parts = [(i, p if i == 0 else pl.ds(0, sources[i].shape[0])) for i, p in parts]
    into = [
        pltpu.make_async_copy(sources[i].at[p], held[i].at[p], sem_in.at[k]) for k, (i, p) in enumerate(parts)
    ]
    out = [
        pltpu.make_async_copy(held[i].at[p], targets[i].at[p], sem_out.at[k]) for k, (i, p) in enumerate(parts)
    ]
    for one in into:
        one.start()
    for first, second in zip(into, out):
        first.wait()
        second.start()
    for one in out:
        one.wait()


def body(q, k, v, h, w, pk, pv, group, length, owner):
    def out(a):
        return jax.ShapeDtypeStruct(a.shape, a.dtype)

    any_, smem = (pl.BlockSpec(memory_space=m) for m in (pl.ANY, pltpu.SMEM))
    dma = pltpu.SemaphoreType.DMA
    outs = (out(q), out(k), out(v), out(pk), out(pv))
    grads = pl.pallas_call(
        kernel,
        out_shape=outs,
        in_specs=[smem] * 3 + [any_] * 7,
        out_specs=(any_,) * 5,
        scratch_shapes=[
            pltpu.VMEM((RESP * LEN, 8 * SHARD), bf16),
            pltpu.VMEM((HEADS_DEV * HD, 8 * SHARD), bf16),
            pltpu.VMEM((RESP * LEN, HEADS_DEV * HD), bf16),
            pltpu.VMEM((RESP * LEN, HEADS_DEV * HD), bf16),
            pltpu.VMEM((RESP * LEN, HEADS_DEV * HD), bf16),
            pltpu.VMEM((RESP * LEN, HD), bf16),
            pltpu.VMEM((RESP * LEN, HD), bf16),
            pltpu.VMEM((RESP * LEN, HD), bf16),
            pltpu.VMEM((RESP * LEN, HD), bf16),
            pltpu.VMEM((2, 8, 2, PROMPT + EXTRA, HD), bf16),
            pltpu.VMEM((KEYS, HD), bf16),
            pltpu.VMEM((KEYS, HD), bf16),
            pltpu.VMEM((HD, KEYS), bf16),
            pltpu.VMEM((HEADS_DEV * HD, LEN), f32),
            pltpu.VMEM((HALVES, KEYS, WIDE), f32),
            pltpu.VMEM((HALVES, KEYS, WIDE), bf16),
            pltpu.VMEM((HALVES, KEYS, WIDE), bf16),
            pltpu.VMEM((KEYS, HD), f32),
            pltpu.VMEM((KEYS, HD), f32),
            pltpu.VMEM((RESP, 2, N_DP, PIECE, HD), bf16),
            pltpu.VMEM((RESP, N_DP, PIECE, HD), bf16),
            pltpu.VMEM((RESP, N_DP, PIECE, HD), bf16),
            pltpu.VMEM((2, N_DP, PIECE, HD), bf16),
            pltpu.VMEM((2, PROMPT, HD), bf16),
            pltpu.VMEM((64, 128), jnp.int32),
            pltpu.SMEM((64, 128), jnp.int32),
            dma((7,)), dma((RESP, 3)), dma((RESP, 14)), dma((RESP, 14)), dma((11,)), dma((11,)),
            dma((RESP, 2)), dma((RESP, 2)), dma((2,)), dma((2,)),
        ],
        compiler_params=pltpu.CompilerParams(
            collective_id=0, has_side_effects=True, vmem_limit_bytes=60 * 2**20
        ),
        cost_estimate=pl.CostEstimate(flops=19 * 10**9, bytes_accessed=20 * 10**6, transcendentals=6 * 10**6),
        name="attention_backward",
    )(group, length, owner, q, k, v, h, w, pk, pv)
    return pl.pallas_call(
        hand_over,
        out_shape=outs,
        in_specs=[any_] * 5,
        out_specs=(any_,) * 5,
        scratch_shapes=[pltpu.VMEM(a.shape, a.dtype) for a in outs] + [dma((8,)), dma((8,))],
        compiler_params=pltpu.CompilerParams(vmem_limit_bytes=60 * 2**20),
        name="hand_over",
    )(*grads)


def solution(mesh):
    whole = P("dp", "tensor")
    return jax.shard_map(
        body,
        mesh=mesh,
        in_specs=(whole, whole, whole, whole, P("tensor", None), whole, whole, P("dp"), P("dp"), P()),
        out_specs=(whole,) * 5,
        check_vma=False,
    )
```

profile of v0, /device:TPU:0, one launch (start us, length us, event | category | flops | bytes accessed | tf_op | source)
XLA Modules:
  0.0 109.4 jit_solution(8088638541015205536)
XLA Ops:
  0.6 106.0 %attention_backward.1 = (bf16[1024,1024]{1,0:T(8,128)(2,1)}, bf16[1024,128]{1,0:T(8,128)(2,1)}, bf16[1024,128]{1,0:T(8,128)(2,1)}, bf16[512,128]{1,0:T(8,128)(2,1)}, bf16[512,128]{1,0:T(8,128)(2,1)}) custom-call(s32[4]{0:T(128)} %group_ref.1, s32[4]{0:T(128)} %length_ref.1, s32[16]{0:T(128)} %owner_ref.1, bf16[1024,1024]{1,0:T(8,128)(2,1)} %q_in.1, ...), custom_call_target="tpu_custom_call" | custom-call | flops 19000000512 | bytes 20000000 | tf_op jit(solution)/shard_map/attention_backward/pallas_call | solution.py:406
  106.6 2.7 %hand_over.1 = (bf16[1024,1024]{1,0:T(8,128)(2,1)}, bf16[1024,128]{1,0:T(8,128)(2,1)}, bf16[1024,128]{1,0:T(8,128)(2,1)}, bf16[512,128]{1,0:T(8,128)(2,1)}, bf16[512,128]{1,0:T(8,128)(2,1)}) custom-call(bf16[1024,1024]{1,0:T(8,128)(2,1)} %get-tuple-element.10.refs_0_, bf16[1024,128]{1,0:T(8,128)(2,1)} %get-tuple-element.11.refs_1_, ...), custom_call_target="tpu_custom_call" | custom-call | tf_op jit(solution)/shard_map/hand_over/pallas_call | solution.py:447
where the time goes:
time: 111 us; the launch traced here: 109 us
  Pallas kernels  109 us (98%)
    pallas_call x1, Pallas kernels, body(): pl.pallas_call(kernel, out_shape=outs, in_specs=[smem] * 3 + [any_] * 7,...  106 us
    pallas_call x1, Pallas kernels, body(): pl.pallas_call(hand_over, out_shape=outs, in_specs=[any_] * 5, out_specs=...  2.74 us

commit v1 on v0

--- a/solution.py
+++ b/solution.py
@@ -19,6 +19,7 @@
 EXTRA = 16
 HPI = 4
 HALVES = HEADS_DEV // HPI
+HALF = LEN // 2
 WIDE = HPI * LEN
 SCALE = HD ** (-0.5)
 SCALE_LOG2E = SCALE * 1.4426950408889634
@@ -101,9 +102,12 @@
 
     nz = 1 - zl
     messages = [
-        (ten, far(zl, y - 1), 0, LEN, t_plus),
-        (ten, far(zl, y + 1), 0, LEN, t_minus),
-        (ten, t_z, 0, LEN, t_z),
+        (ten, far(zl, y - 1), 0, HALF, t_plus),
+        (ten, far(zl, y + 1), 0, HALF, t_minus),
+        (ten, t_z, 0, HALF, t_z),
+        (ten, far(zl, y - 1), HALF, LEN, t_plus),
+        (ten, far(zl, y + 1), HALF, LEN, t_minus),
+        (ten, t_z, HALF, LEN, t_z),
         (t_z, far(nz, y - 1), 0, CUT_P, t_plus),
         (t_z, far(nz, y + 1), 0, CUT_P, t_minus),
         (t_minus, far(zl, y + 2), CUT_LO, CUT_HI, t_plus),
@@ -116,13 +120,13 @@
         (far(zl, y + 2), far(nz, y + 2), CUT_P, CUT_HI, t_z),
         (far(zl, y + 2), far(nz, y + 2), CUT_HI, LEN, t_z),
     ]
-    steps = ((0, 3), (3, 10), (10, 14))
+    steps = ((0, 6), (6, 13), (13, 17))
 
     def part(c, shard, lo, hi):
         return dh.at[pl.ds(pl.multiple_of(c * LEN + lo, 16), hi - lo), cols(shard)]
 
-    def h_send(c, step):
-        for m in range(*steps[step]):
+    def h_send(c, step, some=None):
+        for m in range(*(some or steps[step])):
             source, _, lo, hi, target = messages[m]
             block = part(c, source, lo, hi)
             send(block, block, d_send.at[c, m], d_recv.at[c, m], "tensor", target)
@@ -184,11 +188,11 @@
     p_go(5, 6)
     h_wait(0, 0)
     h_send(0, 1)
+    h_send(2, 0, (0, 3))
     p_wait(0)
     p_go(3, 4)
 
     h_wait(1, 0)
-    h_send(2, 0)
     p_wait(3, 4)
     p_go(7, 8)
     p_wait(5, 6)
@@ -196,6 +200,8 @@
     h_wait(0, 1)
     h_send(0, 2)
     h_send(1, 1)
+    h_send(2, 0, (3, 6))
+    h_send(3, 0, (0, 3))
     p_wait(7, 8)
     p_go(10)
     for one in mine[3:]:
@@ -222,19 +228,6 @@
     causal = key_at <= row_at
     t_at = lax.broadcasted_iota(jnp.int32, (HEADS_DEV * HD, LEN), 1)
 
-    t_last = far(nz, y + 2)
-
-    def gather_part(c):
-        rows = pl.ds(pl.multiple_of(c * LEN, LEN), LEN)
-        gacc[...] = jnp.zeros_like(gacc)
-
-        @pl.loop(1, 8)
-        def _(n):
-            t_ = cols(lax.rem(t_last + n, 8))
-            gacc[...] += dotf(w[:, t_], dh[rows, t_], NT)
-
-    gather_part(0)
-
     def give(c, i):
         spread(lambda k: ctr.at[c, i, k], (rbk, rbv)[i].at[c, dp], a_send.at[c, i], a_recv.at[c, i])
 
@@ -260,100 +253,137 @@
             def _():
                 pltpu.make_async_copy(fin.at[i, s], landing, f_recv.at[i]).start()
 
-    @pl.loop(0, RESP)
-    def _(c):
-        rows = pl.ds(pl.multiple_of(c * LEN, LEN), LEN)
-
-        def heads(ref, h):
-            return jnp.concatenate(
-                [ref[rows, pl.ds(pl.multiple_of((h * HPI + i) * HD, HD), HD)] for i in range(HPI)], 0
-            )
-
-        length = length_ref[c]
+    def rows_of(c):
+        return pl.ds(pl.multiple_of(c * LEN, LEN), LEN)
+
+    def heads(ref, c, h):
+        return jnp.concatenate(
+            [ref[rows_of(c), pl.ds(pl.multiple_of((h * HPI + i) * HD, HD), HD)] for i in range(HPI)], 0
+        )
+
+    def load_keys(c):
         slot = owner_ref[group_ref[c]]
         spot_slot = lax.shift_right_logical(slot, 1) & 7
         ka[0:PROMPT] = tab[0, spot_slot, slot & 1, 0:PROMPT]
         va[0:PROMPT] = tab[1, spot_slot, slot & 1, 0:PROMPT]
-        ka[PROMPT:KEYS] = ko[rows]
-        va[PROMPT:KEYS] = vo[rows]
+        ka[PROMPT:KEYS] = ko[rows_of(c)]
+        va[PROMPT:KEYS] = vo[rows_of(c)]
         kt[...] = ka[...].astype(f32).T.astype(bf16)
-        dka[...] = jnp.zeros_like(dka)
-        dva[...] = jnp.zeros_like(dva)
-
-        @pl.loop(0, HALVES)
-        def _(h):
-            s = dotf(ka[...], heads(q, h), NT)
-            so = jnp.where(causal, s[PROMPT:], -jnp.inf)
-            sp = s[:PROMPT]
-            m = jnp.maximum(jnp.max(sp, 0, keepdims=True), jnp.max(so, 0, keepdims=True))
-            ep = jnp.exp2((sp - m) * SCALE_LOG2E)
-            eo = jnp.exp2((so - m) * SCALE_LOG2E)
-            inv = 1.0 / (jnp.sum(ep, 0, keepdims=True) + jnp.sum(eo, 0, keepdims=True))
-            p = jnp.concatenate([ep * inv, eo * inv], 0)
-            pb[h] = p
-            prb[h] = p.astype(bf16)
-
-        h_wait(c, 2)
-
-        @pl.when(c <= 1)
-        def _():
-            h_wait(c + 2, 0)
-
-        @pl.when(c == 0)
-        def _():
-            h_send(3, 0)
-
-        grad = gacc[...] + dotf(w[:, cols(t_last)], dh[rows, cols(t_last)], NT)
-        g[rows, :] = jnp.where(t_at < length, grad, 0.0).T.astype(bf16)
-
-        @pl.loop(0, HALVES)
-        def _(h):
-            dva[...] += dotf(prb[h], heads(g, h))
-
-        ctr[c, 1] = dva[0:PROMPT].astype(bf16).reshape(N_DP, PIECE, HD)
-        give(c, 1)
-
-        @pl.loop(0, HALVES)
-        def _(h):
-            d = dotf(va[...], heads(g, h), NT)
-            delta = jnp.sum(prb[h].astype(f32) * d, 0, keepdims=True)
-            ds = (pb[h] * (d - delta)).astype(bf16)
-            dsb[h] = ds
-            dka[...] += dotf(ds, heads(q, h))
-
-        ctr[c, 0] = (dka[0:PROMPT] * SCALE).astype(bf16).reshape(N_DP, PIECE, HD)
-        give(c, 0)
-
-        @pl.when(c <= 2)
-        def _():
-            h_wait(c + 1, 1)
-            h_send(c + 1, 2)
-
-        @pl.when(c <= 1)
-        def _():
-            h_send(c + 2, 1)
-
-        @pl.when(c <= 2)
-        def _():
-            gather_part(c + 1)
-
-        @pl.when(c == RESP - 1)
-        def _():
-            to_s.wait()
-            add_up(1)
-
-        @pl.loop(0, HALVES)
-        def _(h):
-            dqt = dotf(kt[...], dsb[h]) * SCALE
-            for i in range(HPI):
-                head = pl.ds(pl.multiple_of((h * HPI + i) * HD, HD), HD)
-                dq[rows, head] = dqt[:, i * LEN : (i + 1) * LEN].T.astype(bf16)
-
+
+    def probs(c, h):
+        s = dotf(ka[...], heads(q, c, h), NT)
+        so = jnp.where(causal, s[PROMPT:], -jnp.inf)
+        sp = s[:PROMPT]
+        m = jnp.maximum(jnp.max(sp, 0, keepdims=True), jnp.max(so, 0, keepdims=True))
+        ep = jnp.exp2((sp - m) * SCALE_LOG2E)
+        eo = jnp.exp2((so - m) * SCALE_LOG2E)
+        inv = 1.0 / (jnp.sum(ep, 0, keepdims=True) + jnp.sum(eo, 0, keepdims=True))
+        return jnp.concatenate([ep * inv, eo * inv], 0)
+
+    def dscore(c, h, p, pr):
+        d = dotf(va[...], heads(g, c, h), NT)
+        delta = jnp.sum(pr.astype(f32) * d, 0, keepdims=True)
+        return (p * (d - delta)).astype(bf16)
+
+    def query_grad(c, h, ds):
+        dqt = dotf(kt[...], ds) * SCALE
+        for i in range(HPI):
+            head = pl.ds(pl.multiple_of((h * HPI + i) * HD, HD), HD)
+            dq[rows_of(c), head] = dqt[:, i * LEN : (i + 1) * LEN].T.astype(bf16)
+
+    def shards(c, *which):
+        return sum(dotf(w[:, cols(t_)], dh[rows_of(c), cols(t_)], NT) for t_ in which)
+
+    def grad_rows(c, grad):
+        g[rows_of(c), :] = jnp.where(t_at < length_ref[c], grad, 0.0).T.astype(bf16)
+
+    def pieces(c, i, total):
+        ctr[c, i] = total.astype(bf16).reshape(N_DP, PIECE, HD)
+        give(c, i)
+
+    def results(c):
+        rows = rows_of(c)
         dko[rows] = (dka[PROMPT:KEYS] * SCALE).astype(bf16)
         dvo[rows] = dva[PROMPT:KEYS].astype(bf16)
         for n, (block, out) in enumerate(((dq, dq_out), (dko, dk_out), (dvo, dv_out))):
             pltpu.make_async_copy(block.at[rows], out.at[rows], osem.at[c, n]).start()
 
+    final = RESP - 1
+    load_keys(final)
+
+    @pl.loop(0, HALVES)
+    def _(h):
+        p = probs(final, h)
+        pb[h] = p
+        prb[h] = p.astype(bf16)
+
+    @pl.loop(0, final)
+    def _(c):
+        load_keys(c)
+        dka[...] = jnp.zeros_like(dka)
+        dva[...] = jnp.zeros_like(dva)
+        h_wait(c, 2)
+        grad_rows(c, dotf(w[...], dh[rows_of(c), :], NT))
+
+        @pl.loop(0, HALVES)
+        def _(h):
+            p = probs(c, h)
+            pr = p.astype(bf16)
+            ds = dscore(c, h, p, pr)
+            dva[...] += dotf(pr, heads(g, c, h))
+            dka[...] += dotf(ds, heads(q, c, h))
+            query_grad(c, h, ds)
+
+            @pl.when(h == 0)
+            def _():
+                h_wait(c + 1, 1)
+                h_send(c + 1, 2)
+
+        @pl.when(c <= 1)
+        def _():
+            h_wait(c + 2, 0)
+            h_send(c + 2, 1)
+
+        @pl.when(c == 0)
+        def _():
+            h_send(final, 0, (3, 6))
+
+        pieces(c, 1, dva[0:PROMPT])
+        pieces(c, 0, dka[0:PROMPT] * SCALE)
+        results(c)
+
+        @pl.when(c == 1)
+        def _():
+            gacc[...] = shards(final, ten, t_plus, t_minus, t_z)
+
+    gacc[...] += shards(final, far(zl, y + 2), far(nz, y - 1), far(nz, y + 1))
+    load_keys(final)
+    dka[...] = jnp.zeros_like(dka)
+    dva[...] = jnp.zeros_like(dva)
+    h_wait(final, 2)
+    grad_rows(final, gacc[...] + shards(final, far(nz, y + 2)))
+
+    @pl.loop(0, HALVES)
+    def _(h):
+        dva[...] += dotf(prb[h], heads(g, final, h))
+
+    pieces(final, 1, dva[0:PROMPT])
+
+    @pl.loop(0, HALVES)
+    def _(h):
+        ds = dscore(final, h, pb[h], prb[h])
+        dsb[h] = ds
+        dka[...] += dotf(ds, heads(q, final, h))
+
+    pieces(final, 0, dka[0:PROMPT] * SCALE)
+    to_s.wait()
+    add_up(1)
+
+    @pl.loop(0, HALVES)
+    def _(h):
+        query_grad(final, h, dsb[h])
+
+    results(final)
     add_up(0)
     for c in range(RESP):
         h_done(c)
@@ -435,7 +465,7 @@
             pltpu.VMEM((2, PROMPT, HD), bf16),
             pltpu.VMEM((64, 128), jnp.int32),
             pltpu.SMEM((64, 128), jnp.int32),
-            dma((7,)), dma((RESP, 3)), dma((RESP, 14)), dma((RESP, 14)), dma((11,)), dma((11,)),
+            dma((7,)), dma((RESP, 3)), dma((RESP, 17)), dma((RESP, 17)), dma((11,)), dma((11,)),
             dma((RESP, 2)), dma((RESP, 2)), dma((2,)), dma((2,)),
         ],
         compiler_params=pltpu.CompilerParams(

time: 111 us -> 106 us (0.955)
  Pallas kernels: 109 us -> 104 us
    pallas_call x1, Pallas kernels: 106 us -> 101 us  [body(): pl.pallas_call(kernel, out_shape=outs, in_specs=[smem] * 3 + [any_] * 7,...]
where the time goes in v1:
time: 106 us; the launch traced here: 105 us
  Pallas kernels  104 us (98%)
    pallas_call x1, Pallas kernels, body(): pl.pallas_call(kernel, out_shape=outs, in_specs=[smem] * 3 + [any_] * 7,...  101 us
    pallas_call x1, Pallas kernels, body(): pl.pallas_call(hand_over, out_shape=outs, in_specs=[any_] * 5, out_specs=...  2.74 us

profile of v1, /device:TPU:0, one launch (start us, length us, event | category | flops | bytes accessed | tf_op | source)
XLA Modules:
  0.0 104.6 jit_solution(8667404485084116619)
XLA Ops:
  0.6 101.2 %attention_backward.1 = (bf16[1024,1024]{1,0:T(8,128)(2,1)}, bf16[1024,128]{1,0:T(8,128)(2,1)}, bf16[1024,128]{1,0:T(8,128)(2,1)}, bf16[512,128]{1,0:T(8,128)(2,1)}, bf16[512,128]{1,0:T(8,128)(2,1)}) custom-call(s32[4]{0:T(128)} %group_ref.1, s32[4]{0:T(128)} %length_ref.1, s32[16]{0:T(128)} %owner_ref.1, bf16[1024,1024]{1,0:T(8,128)(2,1)} %q_in.1, ...), custom_call_target="tpu_custom_call" | custom-call | flops 19000000512 | bytes 20000000 | tf_op jit(solution)/shard_map/attention_backward/pallas_call | solution.py:436
  101.9 2.7 %hand_over.1 = (bf16[1024,1024]{1,0:T(8,128)(2,1)}, bf16[1024,128]{1,0:T(8,128)(2,1)}, bf16[1024,128]{1,0:T(8,128)(2,1)}, bf16[512,128]{1,0:T(8,128)(2,1)}, bf16[512,128]{1,0:T(8,128)(2,1)}) custom-call(bf16[1024,1024]{1,0:T(8,128)(2,1)} %get-tuple-element.10.refs_0_, bf16[1024,128]{1,0:T(8,128)(2,1)} %get-tuple-element.11.refs_1_, ...), custom_call_target="tpu_custom_call" | custom-call | tf_op jit(solution)/shard_map/hand_over/pallas_call | solution.py:477

commit v2 on v1

--- a/solution.py
+++ b/solution.py
@@ -27,7 +27,7 @@
 NT = (((1,), (1,)), ((), ()))
 NN = (((1,), (0,)), ((), ()))
 
-CUT_LO, CUT_P, CUT_HI = 80, 176, 192
+CUT_LO, CUT_P, CUT_HI = 80, 160, 208
 
 
 def dotf(a, b, dims=NN):
@@ -36,9 +36,9 @@
 
 def kernel(
     group_ref, length_ref, owner_ref, q_in, k_in, v_in, h_in, w_in, pk_in, pv_in,
-    dq_out, dk_out, dv_out, dpk_out, dpv_out,
-    dh, w, q, g, dq, ko, vo, dko, dvo, tab, ka, va, kt, gacc, pb, prb, dsb, dka, dva, ctr, rbk, rbv, fin, frec, idx_v, idx_s,
-    lsem, osem, d_send, d_recv, p_send, p_recv, a_send, a_recv, f_send, f_recv,
+    dq, dko, dvo, dpk, dpv,
+    dh, w, q, g, ko, vo, tab, ka, va, kt, gacc, pb, prb, dsb, dka, dva, ctr, rbk, rbv, fin, frec, idx_v, idx_s,
+    lsem, d_send, d_recv, p_send, p_recv, a_send, a_recv, f_send, f_recv,
 ):
     dp = lax.axis_index("dp")
     ten = lax.axis_index("tensor")
@@ -181,17 +181,16 @@
             send(block(peer), landing, ss, rs, "dp", peer)
         pltpu.make_async_copy(block(dp), landing, rs).start()
 
+    h_send(0, 0)
     p_go(0, 1, 2)
-    h_send(0, 0)
     h_send(1, 0)
     p_wait(1, 2)
     p_go(5, 6)
+    p_wait(0)
+    p_go(3, 4)
     h_wait(0, 0)
     h_send(0, 1)
     h_send(2, 0, (0, 3))
-    p_wait(0)
-    p_go(3, 4)
-
     h_wait(1, 0)
     p_wait(3, 4)
     p_go(7, 8)
@@ -305,18 +304,8 @@
         rows = rows_of(c)
         dko[rows] = (dka[PROMPT:KEYS] * SCALE).astype(bf16)
         dvo[rows] = dva[PROMPT:KEYS].astype(bf16)
-        for n, (block, out) in enumerate(((dq, dq_out), (dko, dk_out), (dvo, dv_out))):
-            pltpu.make_async_copy(block.at[rows], out.at[rows], osem.at[c, n]).start()
 
     final = RESP - 1
-    load_keys(final)
-
-    @pl.loop(0, HALVES)
-    def _(h):
-        p = probs(final, h)
-        pb[h] = p
-        prb[h] = p.astype(bf16)
-
     @pl.loop(0, final)
     def _(c):
         load_keys(c)
@@ -352,6 +341,16 @@
         pieces(c, 0, dka[0:PROMPT] * SCALE)
         results(c)
 
+        @pl.when(c == 0)
+        def _():
+            load_keys(final)
+
+            @pl.loop(0, HALVES)
+            def _(h):
+                p = probs(final, h)
+                pb[h] = p
+                prb[h] = p.astype(bf16)
+
         @pl.when(c == 1)
         def _():
             gacc[...] = shards(final, ten, t_plus, t_minus, t_z)
@@ -389,40 +388,21 @@
         h_done(c)
         for i in range(2):
             landed(ctr.at[c, i, 0:15], a_send.at[c, i])
-        done = pl.ds(c * LEN, LEN)
-        for n, (block, out) in enumerate(((dq, dq_out), (dko, dk_out), (dvo, dv_out))):
-            pltpu.make_async_copy(block.at[done], out.at[done], osem.at[c, n]).wait()
     for m, (block, _, _) in enumerate(prompts):
         landed(block, p_send.at[m])
-    last = [
-        pltpu.make_async_copy(frec.at[1], dpv_out, lsem.at[1]),
-        pltpu.make_async_copy(frec.at[0], dpk_out, lsem.at[2]),
-    ]
-    for i in (1, 0):
+    for i, out in ((1, dpv), (0, dpk)):
         landed(frec.at[i], f_recv.at[i])
-        last[1 - i].start()
-    for i in (1, 0):
+        out[...] = frec[i]
+    for i in range(2):
         landed(fin.at[i, 0:15], f_send.at[i])
-        last[1 - i].wait()
 
 
 def hand_over(*refs):
-    n = (len(refs) - 2) // 3
-    sources, targets, held, sem_in, sem_out = refs[:n], refs[n : 2 * n], refs[2 * n : 3 * n], refs[-2], refs[-1]
-    parts = [(i, pl.ds(k * LEN, LEN)) for i in range(n) for k in range(sources[i].shape[0] // LEN if i == 0 else 1)]
-    parts = [(i, p if i == 0 else pl.ds(0, sources[i].shape[0])) for i, p in parts]
-    into = [
-        pltpu.make_async_copy(sources[i].at[p], held[i].at[p], sem_in.at[k]) for k, (i, p) in enumerate(parts)
-    ]
-    out = [
-        pltpu.make_async_copy(held[i].at[p], targets[i].at[p], sem_out.at[k]) for k, (i, p) in enumerate(parts)
-    ]
-    for one in into:
+    n = len(refs) // 2
+    copies = [pltpu.make_async_copy(refs[i], refs[n + i], refs[-1].at[i]) for i in range(n)]
+    for one in copies:
         one.start()
-    for first, second in zip(into, out):
-        first.wait()
-        second.start()
-    for one in out:
+    for one in copies:
         one.wait()
 
 
@@ -430,22 +410,19 @@
     def out(a):
         return jax.ShapeDtypeStruct(a.shape, a.dtype)
 
-    any_, smem = (pl.BlockSpec(memory_space=m) for m in (pl.ANY, pltpu.SMEM))
+    any_, vmem, smem = (pl.BlockSpec(memory_space=m) for m in (pl.ANY, pltpu.VMEM, pltpu.SMEM))
     dma = pltpu.SemaphoreType.DMA
     outs = (out(q), out(k), out(v), out(pk), out(pv))
     grads = pl.pallas_call(
         kernel,
-        out_shape=outs,
+        out_shape=tuple(pltpu.VMEM(a.shape, a.dtype) for a in outs),
         in_specs=[smem] * 3 + [any_] * 7,
-        out_specs=(any_,) * 5,
+        out_specs=(vmem,) * 5,
         scratch_shapes=[
             pltpu.VMEM((RESP * LEN, 8 * SHARD), bf16),
             pltpu.VMEM((HEADS_DEV * HD, 8 * SHARD), bf16),
             pltpu.VMEM((RESP * LEN, HEADS_DEV * HD), bf16),
             pltpu.VMEM((RESP * LEN, HEADS_DEV * HD), bf16),
-            pltpu.VMEM((RESP * LEN, HEADS_DEV * HD), bf16),
-            pltpu.VMEM((RESP * LEN, HD), bf16),
-            pltpu.VMEM((RESP * LEN, HD), bf16),
             pltpu.VMEM((RESP * LEN, HD), bf16),
             pltpu.VMEM((RESP * LEN, HD), bf16),
             pltpu.VMEM((2, 8, 2, PROMPT + EXTRA, HD), bf16),
@@ -465,11 +442,11 @@
             pltpu.VMEM((2, PROMPT, HD), bf16),
             pltpu.VMEM((64, 128), jnp.int32),
             pltpu.SMEM((64, 128), jnp.int32),
-            dma((7,)), dma((RESP, 3)), dma((RESP, 17)), dma((RESP, 17)), dma((11,)), dma((11,)),
+            dma((7,)), dma((RESP, 17)), dma((RESP, 17)), dma((11,)), dma((11,)),
             dma((RESP, 2)), dma((RESP, 2)), dma((2,)), dma((2,)),
         ],
         compiler_params=pltpu.CompilerParams(
-            collective_id=0, has_side_effects=True, vmem_limit_bytes=60 * 2**20
+            collective_id=0, has_side_effects=True, vmem_limit_bytes=56 * 2**20
         ),
         cost_estimate=pl.CostEstimate(flops=19 * 10**9, bytes_accessed=20 * 10**6, transcendentals=6 * 10**6),
         name="attention_backward",
@@ -477,12 +454,12 @@
     return pl.pallas_call(
         hand_over,
         out_shape=outs,
-        in_specs=[any_] * 5,
+        in_specs=[vmem] * 5,
         out_specs=(any_,) * 5,
-        scratch_shapes=[pltpu.VMEM(a.shape, a.dtype) for a in outs] + [dma((8,)), dma((8,))],
-        compiler_params=pltpu.CompilerParams(vmem_limit_bytes=60 * 2**20),
+        scratch_shapes=[dma((5,))],
+        compiler_params=pltpu.CompilerParams(vmem_limit_bytes=4 * 2**20),
         name="hand_over",
-    )(*grads)
+    )(*(pltpu.with_memory_space_constraint(a, pltpu.VMEM) for a in grads))
 
 
 def solution(mesh):

time: 106 us -> 102 us (0.962)
  Pallas kernels: 104 us -> 101 us
    pallas_call x2, Pallas kernels: 104 us -> 101 us  [the longest x1 99.1 us: body(): pl.pallas_call(kernel, out_shape=tuple((pltpu.VMEM(a.shape, a.dtype) for...]
where the time goes in v2:
time: 102 us; the launch traced here: 101 us
  Pallas kernels  101 us (99%)
    pallas_call x1, Pallas kernels, body(): pl.pallas_call(kernel, out_shape=tuple((pltpu.VMEM(a.shape, a.dtype) for...  99.1 us

profile of v2, /device:TPU:0, one launch (start us, length us, event | category | flops | bytes accessed | tf_op | source)
XLA Modules:
  0.0 101.3 jit_solution(4494052386565489642)
XLA Ops:
  0.6 99.1 %attention_backward.1 = (bf16[1024,1024]{1,0:T(8,128)(2,1)S(1)}, bf16[1024,128]{1,0:T(8,128)(2,1)S(1)}, bf16[1024,128]{1,0:T(8,128)(2,1)S(1)}, bf16[512,128]{1,0:T(8,128)(2,1)S(1)}, bf16[512,128]{1,0:T(8,128)(2,1)S(1)}) custom-call(s32[4]{0:T(128)} %group_ref.1, s32[4]{0:T(128)} %length_ref.1, s32[16]{0:T(128)} %owner_ref.1, bf16[1024,1024]{1,0:T(8,128)(2,1)} %q_in.1, ...), custom_call_target="tpu_custom_call" | custom-call | flops 19000000512 | bytes 20000000 | tf_op jit(solution)/shard_map/attention_backward/pallas_call | solution.py:416
  99.7 1.6 %hand_over.1 = (bf16[1024,1024]{1,0:T(8,128)(2,1)}, bf16[1024,128]{1,0:T(8,128)(2,1)}, bf16[1024,128]{1,0:T(8,128)(2,1)}, bf16[512,128]{1,0:T(8,128)(2,1)}, bf16[512,128]{1,0:T(8,128)(2,1)}) custom-call(bf16[1024,1024]{1,0:T(8,128)(2,1)S(1)} %get-tuple-element.10.refs_0_, bf16[1024,128]{1,0:T(8,128)(2,1)S(1)} %get-tuple-element.11.refs_1_, ...), custom_call_target="tpu_custom_call" | custom-call | tf_op jit(solution)/shard_map/hand_over/pallas_call | solution.py:454

commit v3 on v2

--- a/solution.py
+++ b/solution.py
@@ -37,7 +37,7 @@
 def kernel(
     group_ref, length_ref, owner_ref, q_in, k_in, v_in, h_in, w_in, pk_in, pv_in,
     dq, dko, dvo, dpk, dpv,
-    dh, w, q, g, ko, vo, tab, ka, va, kt, gacc, pb, prb, dsb, dka, dva, ctr, rbk, rbv, fin, frec, idx_v, idx_s,
+    dh, w, q, g, ko, vo, tab, ka, va, kt, gacc, pb, prb, dsb, dka, dva, ctr, rbk, rbv, fin, idx_v, idx_s,
     lsem, d_send, d_recv, p_send, p_recv, a_send, a_recv, f_send, f_recv,
 ):
     dp = lax.axis_index("dp")
@@ -242,7 +242,7 @@
                 r = idx_s[s * RESP + k, 0]
                 total += (rbk, rbv)[i][r & (RESP - 1), lax.shift_right_logical(r, 2) & (N_DP - 1)].astype(f32)
             fin[i, s] = total.astype(bf16)
-            landing = frec.at[i, pl.ds(dp * PIECE, PIECE)]
+            landing = (dpk, dpv)[i].at[pl.ds(pl.multiple_of(dp * PIECE, PIECE), PIECE)]
 
             @pl.when(n < N_DP)
             def _():
@@ -391,8 +391,7 @@
     for m, (block, _, _) in enumerate(prompts):
         landed(block, p_send.at[m])
     for i, out in ((1, dpv), (0, dpk)):
-        landed(frec.at[i], f_recv.at[i])
-        out[...] = frec[i]
+        landed(out, f_recv.at[i])
     for i in range(2):
         landed(fin.at[i, 0:15], f_send.at[i])
 
@@ -439,7 +438,6 @@
             pltpu.VMEM((RESP, N_DP, PIECE, HD), bf16),
             pltpu.VMEM((RESP, N_DP, PIECE, HD), bf16),
             pltpu.VMEM((2, N_DP, PIECE, HD), bf16),
-            pltpu.VMEM((2, PROMPT, HD), bf16),
             pltpu.VMEM((64, 128), jnp.int32),
             pltpu.SMEM((64, 128), jnp.int32),
             dma((7,)), dma((RESP, 17)), dma((RESP, 17)), dma((11,)), dma((11,)),

time: 102 us -> 102 us (level)
  no operation moved by 1% of the time
where the time goes in v3:
time: 102 us; the launch traced here: 101 us
  Pallas kernels  101 us (99%)
    pallas_call x1, Pallas kernels, body(): pl.pallas_call(kernel, out_shape=tuple((pltpu.VMEM(a.shape, a.dtype) for...  99.1 us

profile of v3, /device:TPU:0, one launch (start us, length us, event | category | flops | bytes accessed | tf_op | source)
XLA Modules:
  0.0 101.3 jit_solution(5986374738435625391)
XLA Ops:
  0.6 99.1 %attention_backward.1 = (bf16[1024,1024]{1,0:T(8,128)(2,1)S(1)}, bf16[1024,128]{1,0:T(8,128)(2,1)S(1)}, bf16[1024,128]{1,0:T(8,128)(2,1)S(1)}, bf16[512,128]{1,0:T(8,128)(2,1)S(1)}, bf16[512,128]{1,0:T(8,128)(2,1)S(1)}) custom-call(s32[4]{0:T(128)} %group_ref.1, s32[4]{0:T(128)} %length_ref.1, s32[16]{0:T(128)} %owner_ref.1, bf16[1024,1024]{1,0:T(8,128)(2,1)} %q_in.1, ...), custom_call_target="tpu_custom_call" | custom-call | flops 19000000512 | bytes 20000000 | tf_op jit(solution)/shard_map/attention_backward/pallas_call | solution.py:415
  99.7 1.6 %hand_over.1 = (bf16[1024,1024]{1,0:T(8,128)(2,1)}, bf16[1024,128]{1,0:T(8,128)(2,1)}, bf16[1024,128]{1,0:T(8,128)(2,1)}, bf16[512,128]{1,0:T(8,128)(2,1)}, bf16[512,128]{1,0:T(8,128)(2,1)}) custom-call(bf16[1024,1024]{1,0:T(8,128)(2,1)S(1)} %get-tuple-element.10.refs_0_, bf16[1024,128]{1,0:T(8,128)(2,1)S(1)} %get-tuple-element.11.refs_1_, ...), custom_call_target="tpu_custom_call" | custom-call | tf_op jit(solution)/shard_map/hand_over/pallas_call | solution.py:452
